TPU v7x, 128 devices: a whole 4x4x4 slice. The times are simulated.
128 devices in a mesh: section: 8 (over x, y_lo), seq: 16 (over z, y_hi, core).
Axes of the slice: x: 4, y: 4 (y_hi: 2, y_lo: 2; y = y_hi * 2 + y_lo), z: 4, core: 2. Of those that a mesh axis runs over, the one named last changes fastest.
Arguments:
- inflow: bfloat16 [8, 1024, 4096], P('section', 'seq'), may hold values from -6 to 6
- fresh: bfloat16 [1, 1024, 4096], P(None, 'seq'), may hold values from -6 to 6
- proj_weight: bfloat16 [8, 4096, 640], P('section'), may hold values from -0.09375 to 0.09375
- xz_weight: bfloat16 [8, 4096, 2, 4096], P('section', None, None, 'seq'), may hold values from -0.09375 to 0.09375
- conv_weight: float32 [8, 4, 4608], P('section'), may hold values from -3 to 3
- conv_bias: float32 [8, 4608], P('section'), may hold values from -3 to 3
- step_bias: float32 [8, 128], P('section'), may hold values from -3 to 0
- decay_log: float32 [8, 128], P('section'), may hold values from -7 to -1
- skip_weight: float32 [8, 128], P('section'), may hold values from 0.5 to 1.5
- norm_gain: float32 [8, 4096], P('section'), may hold values from 0.5 to 1.5
- out_weight: bfloat16 [8, 4096, 4096], P('section', 'seq'), may hold values from -0.09375 to 0.09375
Outputs:
- section_outputs: float32 [8, 2, 1024, 4096], P('section', None, 'seq')
All inputs are finite; a program needn't handle non-finite values.
Results may differ from a plain program's by a relative error of at most 0.014.
Values may be sent and summed in bfloat16 or wider, within the bound.
A program may use at most 128 MiB of HBM per device.

v0:
```python
import jax
import jax.numpy as jnp
from jax import lax
from jax.sharding import PartitionSpec as P

HEADS = 128
HEAD_DIM = 32
STATE = 64
GROUPS = 4
CONV = 4
BLOCK = 128


def shifted(value, axis, steps):
    count = lax.axis_size(axis)
    leading, last = (max(0, -steps), min(count, count - steps))
    return lax.ppermute(value, axis, [(source, source + steps) for source in range(leading, last)])


def run_block(state, pieces):
    x_block, b_block, c_block, step_block, decay_block = pieces
    cumulus = jnp.cumsum(decay_block, axis=0)
    scores = jnp.einsum("qgn,kgn->gqk", c_block, b_block, preferred_element_type=jnp.float32)
    along = jnp.moveaxis(cumulus, 0, 2)
    row_count = cumulus.shape[0]
    row_index = lax.broadcasted_iota(jnp.int32, (row_count, row_count), 0)
    col_index = lax.broadcasted_iota(jnp.int32, (row_count, row_count), 1)
    log_gap = jnp.where(row_index >= col_index, along[..., :, None] - along[..., None, :], -1e30)
    step_along = jnp.moveaxis(step_block, 0, 2)
    mixing = (scores[:, None] * jnp.exp(log_gap) * step_along[..., None, :]).astype(jnp.bfloat16)
    diagonal_out = jnp.einsum(
        "gjqk,kgjp->qgjp", mixing, x_block, preferred_element_type=jnp.float32
    )
    block_total = cumulus[-1]
    weighted = (
        x_block.astype(jnp.float32) * (jnp.exp(block_total[None] - cumulus) * step_block)[..., None]
    ).astype(jnp.bfloat16)
    block_state = jnp.einsum(
        "kgjp,kgn->gjpn", weighted, b_block, preferred_element_type=jnp.float32
    )
    entering = state.astype(jnp.bfloat16)
    off_out = (
        jnp.einsum("qgn,gjpn->qgjp", c_block, entering, preferred_element_type=jnp.float32)
        * jnp.exp(cumulus)[..., None]
    )
    new_state = jnp.exp(block_total)[..., None, None] * state + block_state
    return (new_state, diagonal_out + off_out)


def on_device(
    inflow,
    fresh,
    proj_weight,
    xz_weight,
    conv_weight,
    conv_bias,
    step_bias,
    decay_log,
    skip_weight,
    norm_gain,
    out_weight,
):
    group_size = lax.axis_size("seq")
    position = lax.axis_index("section")
    member = lax.axis_index("seq")
    tokens, width = (inflow.shape[1], inflow.shape[2])
    length = tokens * group_size
    inner = HEADS * HEAD_DIM
    heads_dev = HEADS // group_size
    chan_dev = heads_dev * HEAD_DIM
    bc_width = GROUPS * STATE
    per_group = HEADS // GROUPS
    head_start = member * heads_dev
    group_index = head_start // per_group
    b_start = group_index * STATE
    c_start = bc_width + group_index * STATE
    dt_start = 2 * bc_width + head_start
    xz_local = xz_weight[0].reshape(width, 2 * chan_dev)
    full_proj = proj_weight[0]

    def own_channels(table):
        last = table.ndim - 1
        return jnp.concatenate(
            [
                lax.dynamic_slice_in_dim(table, head_start * HEAD_DIM, chan_dev, last),
                lax.dynamic_slice_in_dim(table, inner + b_start, STATE, last),
                lax.dynamic_slice_in_dim(table, inner + c_start, STATE, last),
            ],
            axis=last,
        )

    taps_own = own_channels(conv_weight[0])
    offset_own = own_channels(conv_bias[0])
    bias_own = lax.dynamic_slice_in_dim(step_bias[0], head_start, heads_dev)
    rate_own = -jnp.exp(lax.dynamic_slice_in_dim(decay_log[0], head_start, heads_dev))
    skip_own = lax.dynamic_slice_in_dim(skip_weight[0], head_start, heads_dev)
    gain_own = lax.dynamic_slice_in_dim(norm_gain[0], head_start * HEAD_DIM, chan_dev)
    out_local = out_weight[0]
    group_mask = (lax.broadcasted_iota(jnp.int32, (GROUPS, 1), 0) == group_index).astype(
        jnp.float32
    )
    own_weight = jnp.concatenate(
        [
            xz_local,
            lax.dynamic_slice_in_dim(full_proj, b_start, STATE, 1),
            lax.dynamic_slice_in_dim(full_proj, c_start, STATE, 1),
            lax.dynamic_slice_in_dim(full_proj, dt_start, heads_dev, 1),
        ],
        axis=1,
    )

    def layer(shard):
        projected = jnp.dot(
            lax.all_gather(shard, "seq", axis=0, tiled=True),
            own_weight,
            preferred_element_type=jnp.float32,
        ).astype(jnp.bfloat16)
        gate_z = projected[:, :chan_dev]
        joined = projected[:, chan_dev : 2 * chan_dev + 2 * STATE]
        padded = jnp.concatenate(
            [jnp.zeros((CONV - 1, joined.shape[1]), jnp.bfloat16), joined], axis=0
        )
        conv_sum = offset_own + taps_own[0] * padded[0:length].astype(jnp.float32)
        for offset in range(1, CONV):
            conv_sum = conv_sum + taps_own[offset] * padded[offset : offset + length].astype(
                jnp.float32
            )
        convolved = jax.nn.silu(conv_sum).astype(jnp.bfloat16)
        block_count = length // BLOCK
        x_part = convolved[:, :chan_dev]
        x_blocks = x_part.reshape(block_count, BLOCK, 1, heads_dev, HEAD_DIM)
        b_blocks = convolved[:, chan_dev : chan_dev + STATE].reshape(block_count, BLOCK, 1, STATE)
        c_blocks = convolved[:, chan_dev + STATE :].reshape(block_count, BLOCK, 1, STATE)
        step_size = jax.nn.softplus(
            projected[:, 2 * chan_dev + 2 * STATE :].astype(jnp.float32) + bias_own
        )
        log_decay = rate_own * step_size
        step_blocks = step_size.reshape(block_count, BLOCK, 1, heads_dev)
        decay_blocks = log_decay.reshape(block_count, BLOCK, 1, heads_dev)
        start_state = jnp.zeros((1, heads_dev, HEAD_DIM, STATE), jnp.float32)
        _, scanned = lax.scan(
            run_block, start_state, (x_blocks, b_blocks, c_blocks, step_blocks, decay_blocks)
        )
        mixed = scanned.reshape(length, heads_dev, HEAD_DIM) + skip_own[:, None] * x_part.reshape(
            length, heads_dev, HEAD_DIM
        ).astype(jnp.float32)
        gated = mixed.reshape(length, chan_dev) * jax.nn.silu(gate_z.astype(jnp.float32))
        own_squares = jnp.sum(gated * gated, axis=1)
        summed_squares = lax.psum(group_mask * own_squares[None, :], "seq")
        mean_square = jnp.sum(summed_squares * group_mask, axis=0) / (inner // GROUPS)
        normed = (gated * lax.rsqrt(mean_square + 1e-05)[:, None] * gain_own).astype(jnp.bfloat16)
        return lax.psum_scatter(
            jnp.dot(normed, out_local, preferred_element_type=jnp.float32),
            "seq",
            scatter_dimension=0,
            tiled=True,
        )

    results = [layer(inflow[0])]
    passed = shifted(results[-1].astype(jnp.bfloat16), "section", 1)
    entering_rows = jnp.where(position == 0, fresh[0], passed)
    results.append(layer(entering_rows))
    return jnp.stack(results)[None]


def solution(mesh):
    placed = (
        P("section", "seq", None),
        P(None, "seq", None),
        P("section", None, None),
        P("section", None, None, "seq"),
        P("section", None, None),
        P("section", None),
        P("section", None),
        P("section", None),
        P("section", None),
        P("section", None),
        P("section", "seq", None),
    )
    return jax.shard_map(
        on_device,
        mesh=mesh,
        in_specs=placed,
        out_specs=P("section", None, "seq", None),
        check_vma=False,
    )
```

profile of v0, /device:TPU:14, one launch (start us, length us, event | category | flops | bytes accessed | tf_op | source)
XLA Modules:
  0.0 818.7 jit_solution(11342104842031938381)
XLA Ops:
  7.4 4.9 copy.90
  23.3 61.0 %all-gather.6.cloned.1.call-done = bf16[1,1024,4096]{2,1,0:T(8,128)(2,1)} async-done(((bf16[1,64,4096]{2,1,0:T(8,128)(2,1)}), bf16[1,1024,4096]{2,1,0:T(8,128)(2,1)}) %all-gather.6.cloned.1.call-update) | async-done | bytes 8388624 | tf_op jit(solution)/shard_map/all_gather | solution.py:114
  84.3 12.6 %fusion.79 = bf16[1024,648]{0,1:T(8,128)(2,1)S(1)} fusion(bf16[1,1024,4096]{2,1,0:T(8,128)(2,1)} %all-gather.6.cloned.1.call-done, bf16[4096,8]{1,0:T(8,128)(2,1)} %dynamic-slice_bitcast_fusion, bf16[4096,64]{1,0:T(8,128)(2,1)} %get-tuple-element.242, bf16[4096,64]{1,0:T(8,128)(2,1)S(1)} %get-tuple-element.241, bf16[4096,512]{1,0:T(8,128)(2,1)} %bitcast.317), kind=kOutput, calls=%fused_computation.100 | convolution fusion | flops 5457715200 | bytes 15024128 | tf_op jit(solution)/shard_map/dot_general | solution.py:113
  102.7 77.7 %while.26 = (s32[]{:T(128)}, f32[1,8,32,64]{3,2,1,0:T(8,128)S(1)}, f32[8,128,1,8,32]{1,0,4,3,2:T(8,128)}, f32[8,128,1,8]{1,3,0,2:T(8,128)}, bf16[8,128,1,8,32]{1...) while((s32[]{:T(128)}, f32[1,8,32,64]{3,2,1,0:T(8,128)S(1)}, ...), condition=%wide.region_2.3_spmd.clone, body=%wide.region_0.2_spmd.clone.sunk | while | flops 19907588 | bytes 1384216 | solution.py:141
  116.5 4.4 dynamic_update_slice.11
  126.3 4.4 dynamic_update_slice.11
  183.4 66.3 %psum.14 = f32[4,1024]{1,0:T(4,128)S(1)} all-reduce(f32[4,1024]{1,0:T(4,128)S(1)} %broadcast_multiply_fusion.1), channel_id=1, replica_groups=mesh['section'=8,'seq'=16] {'seq'}, use_global_device_ids=true, to_apply=%region_4.5 | all-reduce | flops 4096 | bytes 32768 | tf_op jit(solution)/shard_map/psum | solution.py:149
  249.8 9.4 %fusion.74 = f32[1024,4096]{1,0:T(8,128)} fusion(bf16[1,256,4096]{2,1,0:T(8,128)(2,1)S(1)} %copy-done, f32[1024,256]{0,1:T(8,128)} %get-tuple-element.232, f32[256]{0:T(256)S(1)} %bitcast.331, f32[1024]{0:T(1024)S(1)} %add_rsqrt_fusion.1), kind=kOutput, calls=%fused_computation.94 | convolution fusion | flops 2148270080 | bytes 19928064 | tf_op jit(solution)/shard_map/dot_general | solution.py:153
  259.3 143.2 %reduce-scatter.3.cloned.1.call-done = f32[64,4096]{1,0:T(8,128)} async-done(((f32[1024,4096]{1,0:T(8,128)}), f32[64,4096]{1,0:T(8,128)}) %reduce-scatter.3.cloned.1.call-update) | async-done | bytes 1048592 | tf_op jit(solution)/shard_map/reduce_scatter | solution.py:152
  405.8 14.0 %collective-permute-done = bf16[64,4096]{1,0:T(8,128)(2,1)} collective-permute-done((bf16[64,4096]{1,0:T(8,128)(2,1)}, bf16[64,4096]{1,0:T(8,128)(2,1)}, u32[]{:S(2)}, u32[]{:S(2)}) %collective-permute-start) | collective-permute-done | bytes 524320 | tf_op jit(solution)/shard_map/ppermute | solution.py:17
  422.2 71.0 %all-gather.4.cloned.1.call-done = bf16[1024,4096]{1,0:T(8,128)(2,1)} async-done(((bf16[64,4096]{1,0:T(8,128)(2,1)}), bf16[1024,4096]{1,0:T(8,128)(2,1)}) %all-gather.4.cloned.1.call-update) | async-done | bytes 8388624 | tf_op jit(solution)/shard_map/all_gather | solution.py:114
  493.2 11.0 %convolution_convert_fusion = bf16[1024,648]{0,1:T(8,128)(2,1)S(1)} fusion(bf16[1024,4096]{1,0:T(8,128)(2,1)} %all-gather.4.cloned.1.call-done, bf16[4096,8]{1,0:T(8,128)(2,1)} %dynamic-slice_bitcast_fusion, bf16[4096,64]{1,0:T(8,128)(2,1)} %get-tuple-element.242, bf16[4096,64]{1,0:T(8,128)(2,1)S(1)} %copy-done.5, bf16[4096,512]{1,0:T(8,128)(2,1)} %bitcast.318), kind=kOutput, calls=%fused_computation.97 | convolution fusion | flops 5457715200 | bytes 15024128 | tf_op jit(solution)/shard_map/dot_general | solution.py:113
  509.7 78.0 %while.27 = (s32[]{:T(128)}, f32[1,8,32,64]{3,2,1,0:T(8,128)S(1)}, f32[8,128,1,8,32]{1,0,4,3,2:T(8,128)}, f32[8,128,1,8]{1,3,0,2:T(8,128)}, bf16[8,128,1,8,32]{1...) while((s32[]{:T(128)}, f32[1,8,32,64]{3,2,1,0:T(8,128)S(1)}, ...), condition=%wide.region_9.10_spmd.clone, body=%wide.region_7.9_spmd.clone.sunk | while | flops 19907588 | bytes 1384216 | solution.py:141
  513.8 4.5 dynamic_update_slice.12
  523.6 4.5 dynamic_update_slice.12
  533.3 4.5 dynamic_update_slice.12
  543.1 4.5 dynamic_update_slice.12
  552.8 4.5 dynamic_update_slice.12
  562.6 4.5 dynamic_update_slice.12
  572.3 4.5 dynamic_update_slice.12
  582.1 4.5 dynamic_update_slice.12
  590.7 66.3 %psum.15 = f32[4,1024]{1,0:T(4,128)S(1)} all-reduce(f32[4,1024]{1,0:T(4,128)S(1)} %broadcast_multiply_fusion), channel_id=1, replica_groups=mesh['section'=8,'seq'=16] {'seq'}, use_global_device_ids=true, to_apply=%region_11.12 | all-reduce | flops 4096 | bytes 32768 | tf_op jit(solution)/shard_map/psum | solution.py:149
  657.0 9.5 %fusion.72 = f32[1024,4096]{1,0:T(8,128)} fusion(bf16[1,256,4096]{2,1,0:T(8,128)(2,1)S(1)} %copy-done, f32[1024,256]{0,1:T(8,128)} %get-tuple-element.230, f32[1024]{0:T(1024)S(1)} %add_rsqrt_fusion, f32[256]{0:T(256)S(1)} %bitcast.332), kind=kOutput, calls=%fused_computation.92 | convolution fusion | flops 2148270080 | bytes 19928064 | tf_op jit(solution)/shard_map/dot_general | solution.py:153
  666.5 143.0 %reduce-scatter.5.cloned.1.call-done = f32[64,4096]{1,0:T(8,128)} async-done(((f32[1024,4096]{1,0:T(8,128)}), f32[64,4096]{1,0:T(8,128)}) %reduce-scatter.5.cloned.1.call-update) | async-done | bytes 1048592 | tf_op jit(solution)/shard_map/reduce_scatter | solution.py:152
  (355 shorter events, 147.7 us)
Async XLA Ops:
  6.5 243.2 %copy-start = (bf16[1,256,4096]{2,1,0:T(8,128)(2,1)S(1)}, bf16[1,256,4096]{2,1,0:T(8,128)(2,1)}, u32[]{:S(2)}) copy-start(bf16[1,256,4096]{2,1,0:T(8,128)(2,1)} %param.25) | copy-start | bytes 6291460
  6.5 77.8 %all-gather.6.cloned.1.call-start = ((), (), s32[]{:S(2)}) async-start(), calls=%async_computation.5 | async-start | bytes 8912896 | tf_op jit(solution)/shard_map/all_gather | solution.py:114
  7.3 395.2 %reduce-scatter.3.cloned.1.call-start = ((), (), s32[]{:S(2)}) async-start(), calls=%async_computation.2 | async-start | bytes 17825792 | tf_op jit(solution)/shard_map/reduce_scatter | solution.py:152
  7.3 5.0 copy-start.23
  7.4 7.7 copy-start.21
  7.4 7.7 copy-start.22
  15.1 85.7 %copy-start.17 = (f32[8]{0:T(128)}, f32[8]{0:T(128)S(1)}, u32[]{:S(2)}) copy-start(f32[8]{0:T(128)S(1)} %get-tuple-element.255) | copy-start | bytes 100
  15.1 85.7 %copy-start.19 = (f32[8]{0:T(128)}, f32[8]{0:T(128)S(1)}, u32[]{:S(2)}) copy-start(f32[8]{0:T(128)S(1)} %get-tuple-element.256) | copy-start | bytes 100
  15.9 81.2 %copy-start.12 = (f32[384]{0:T(512)}, f32[384]{0:T(512)S(1)}, u32[]{:S(2)}) copy-start(f32[384]{0:T(512)S(1)} %pad_maximum_fusion.4) | copy-start | bytes 4612
  17.4 79.6 %copy-start.6 = (f32[384]{0:T(512)}, f32[384]{0:T(512)S(1)}, u32[]{:S(2)}) copy-start(f32[384]{0:T(512)S(1)} %get-tuple-element.194) | copy-start | bytes 4612
  17.5 79.6 %copy-start.8 = (f32[384]{0:T(512)}, f32[384]{0:T(512)S(1)}, u32[]{:S(2)}) copy-start(f32[384]{0:T(512)S(1)} %get-tuple-element.195) | copy-start | bytes 4612
  17.5 79.6 %copy-start.10 = (f32[384]{0:T(512)}, f32[384]{0:T(512)S(1)}, u32[]{:S(2)}) copy-start(f32[384]{0:T(512)S(1)} %get-tuple-element.196) | copy-start | bytes 4612
  23.3 73.7 %copy-start.4 = (bf16[4096,64]{1,0:T(8,128)(2,1)}, bf16[4096,64]{1,0:T(8,128)(2,1)S(1)}, u32[]{:S(2)}) copy-start(bf16[4096,64]{1,0:T(8,128)(2,1)S(1)} %get-tuple-element.241) | copy-start | bytes 1572868
  97.0 3.8 copy-start.3
  259.2 234.0 %copy-start.5 = (bf16[4096,64]{1,0:T(8,128)(2,1)S(1)}, bf16[4096,64]{1,0:T(8,128)(2,1)}, u32[]{:S(2)}) copy-start(bf16[4096,64]{1,0:T(8,128)(2,1)} %copy-done.4) | copy-start | bytes 1572868
  259.2 233.9 %all-gather.4.cloned.1.call-start = ((), (), s32[]{:S(2)}) async-start(), calls=%async_computation.3 | async-start | bytes 8912896 | tf_op jit(solution)/shard_map/all_gather | solution.py:114
  404.5 15.3 %collective-permute-start = (bf16[64,4096]{1,0:T(8,128)(2,1)}, bf16[64,4096]{1,0:T(8,128)(2,1)}, u32[]{:S(2)}, u32[]{:S(2)}) collective-permute-start(bf16[64,4096]{1,0:T(8,128)(2,1)} %convert_element_type.138), channel_id=1, source_target_pairs={{0,16},{16,32},{32,48},{48,64},{64,80},{80,96},{96,112},{1,17},{17... | collective-permute-start | bytes 1572872 | tf_op jit(solution)/shard_map/ppermute | solution.py:17
  421.9 387.6 %reduce-scatter.5.cloned.1.call-start = ((), (), s32[]{:S(2)}) async-start(), calls=%async_computation.4 | async-start | bytes 17825792 | tf_op jit(solution)/shard_map/reduce_scatter | solution.py:152
  422.1 82.1 %copy-start.7 = (f32[384]{0:T(512)S(1)}, f32[384]{0:T(512)}, u32[]{:S(2)}) copy-start(f32[384]{0:T(512)} %copy-done.6) | copy-start | bytes 4612
  422.2 82.1 %copy-start.9 = (f32[384]{0:T(512)S(1)}, f32[384]{0:T(512)}, u32[]{:S(2)}) copy-start(f32[384]{0:T(512)} %copy-done.8) | copy-start | bytes 4612
  422.2 82.1 %copy-start.11 = (f32[384]{0:T(512)S(1)}, f32[384]{0:T(512)}, u32[]{:S(2)}) copy-start(f32[384]{0:T(512)} %copy-done.10) | copy-start | bytes 4612
  422.2 82.1 %copy-start.13 = (f32[384]{0:T(512)S(1)}, f32[384]{0:T(512)}, u32[]{:S(2)}) copy-start(f32[384]{0:T(512)} %copy-done.12) | copy-start | bytes 4612
  509.7 78.0 %copy-start.14 = (f32[256]{0:T(256)S(1)}, f32[256]{0:T(256)}, u32[]{:S(2)}) copy-start(f32[256]{0:T(256)} %mul.351) | copy-start | bytes 3076
  666.5 143.0 %copy-start.1 = (f32[64,4096]{1,0:T(8,128)S(1)}, f32[64,4096]{1,0:T(8,128)}, u32[]{:S(2)}) copy-start(f32[64,4096]{1,0:T(8,128)} %reduce-scatter.3.cloned.1.call-done) | copy-start | bytes 3145732
  (5 other events, 11.6 us)
Sparse Core Ops, SparseCore 0:
  9.8 74.4 all-gather.5
  259.4 143.0 reduce-scatter.2
  422.0 71.1 all-gather.3
  666.7 142.7 reduce-scatter.4
where the time goes:
time: 825 us; the launch traced here: 819 us
  waiting for transfers between devices  433 us (52%)
  blocking collectives  133 us (16%)
  local copies, waits for them, and re-layouts  109 us (13%)
  matrix products  107 us (13%)
  other arithmetic  21.6 us (3%)
  between operations  13.6 us (2%)
    reduce_scatter x2, waiting for transfers between devices, layer(): lax.psum_scatter(jnp.dot(normed, out_local, preferred_element_type=jnp.fl...  286 us
    psum x2, blocking collectives, layer(): summed_squares = lax.psum(group_mask * own_squares[None, :], 'seq')  133 us
    all_gather x2, waiting for transfers between devices, layer(): lax.all_gather(shard, 'seq', axis=0, tiled=True)  132 us
    dynamic_update_slice x16, local copies, waits for them, and re-layouts, layer(): lax.scan(run_block, start_state, (x_blocks, b_blocks, c_blocks, step_bloc...  71.3 us
    dot_general x2, matrix products, layer(): jnp.dot(lax.all_gather(shard, 'seq', axis=0, tiled=True), own_weight, pre...  23.6 us
    dot_general x2, matrix products, layer(): jnp.dot(normed, out_local, preferred_element_type=jnp.float32)  18.9 us
    dot_general x16, matrix products, run_block(): jnp.einsum('gjqk,kgjp->qgjp', mixing, x_block, preferred_element_type=jnp...  18.8 us
  transfers between devices with their start and end apart: 5, of which 5 were waited for; matrix products, arithmetic and copies ran while one was open for 2% of the time, Pallas kernels for 0%

commit v1 on v0

v1 whole, which is shorter than its diff:
```python
import functools

import jax
import jax.numpy as jnp
from jax import lax
from jax.experimental import pallas as pl
from jax.experimental.pallas import tpu as pltpu
from jax.sharding import PartitionSpec as P

MESH = pl.DeviceIdType.MESH
F32 = jnp.float32
BF16 = jnp.bfloat16
HIGHEST = lax.Precision.HIGHEST
TOKENS = 1024
WIDTH = 4096
CHAN = 256
BLOCK = 128
PIECE = 32
COLS = 896
MIB = 2**20


def place():
    sec = lax.axis_index("section")
    me = lax.axis_index("seq")
    z, h, c = me // 4, (me // 2) % 2, me % 2
    return sec, z, h, c


class Copies:
    def __init__(self, send_sem, recv_sem):
        self.send_sem, self.recv_sem = send_sem, recv_sem
        self.made = []

    def new(self, src, dst, target):
        index = len(self.made)
        copy = pltpu.make_async_remote_copy(
            src_ref=src,
            dst_ref=dst,
            send_sem=self.send_sem.at[index],
            recv_sem=self.recv_sem.at[index],
            device_id=target,
            device_id_type=MESH,
        )
        copy.start()
        self.made.append(copy)
        return copy

    def finish(self):
        for copy in self.made:
            copy.wait_send()


def meet(targets):
    barrier = pltpu.get_barrier_semaphore()
    for target in targets:
        pl.semaphore_signal(barrier, inc=1, device_id=target, device_id_type=MESH)
    pl.semaphore_wait(barrier, len(targets))


def gather_kernel(shard, wxz, wproj, out, act, weight, send_sem, recv_sem, local_sem):
    sec, z, h, c = place()
    zp, zm, zz, hh = (z + 1) % 4, (z + 3) % 4, (z + 2) % 4, 1 - h

    def dev(z_, h_, c_):
        return (sec, z_ * 4 + h_ * 2 + c_)

    up, down, across, sib = dev(zp, h, c), dev(zm, h, c), dev(z, hh, c), dev(z, h, 1 - c)
    pair = z // 2
    loads = []
    for index, (src, dst) in enumerate(
        [
            (shard, act.at[pl.ds(pl.multiple_of((z * 4 + h * 2 + c) * 64, 64), 64)]),
            (wxz, weight.at[:, pl.ds(0, 2 * CHAN)]),
            (wproj.at[:, pl.ds(pl.multiple_of(pair * 128, 128), 128)], weight.at[:, pl.ds(512, 128)]),
            (wproj.at[:, pl.ds(pl.multiple_of(256 + pair * 128, 128), 128)], weight.at[:, pl.ds(640, 128)]),
            (wproj.at[:, pl.ds(512, 128)], weight.at[:, pl.ds(768, 128)]),
        ]
    ):
        load = pltpu.make_async_copy(src, dst, local_sem.at[index])
        load.start()
        loads.append(load)
    meet([up, down, across, sib])
    copies = Copies(send_sem, recv_sem)

    def rows(z_, h_, p):
        start = pl.multiple_of((z_ * 2 + h_) * 128 + c * 64 + p * PIECE, PIECE)
        return act.at[pl.ds(start, PIECE)]

    def own(p):
        return shard.at[pl.ds(p * PIECE, PIECE)]

    def forward(z_, h_, p, target):
        return copies.new(rows(z_, h_, p), rows(z_, h_, p), target)

    def project(z_, h_):
        start = pl.multiple_of((z_ * 2 + h_) * 128, 128)
        for first, size in ((0, 256), (256, 256), (512, 256), (768, 128)):
            out[pl.ds(start, 128), pl.ds(first, size)] = jnp.dot(
                act[pl.ds(start, 128), :], weight[:, pl.ds(first, size)], preferred_element_type=F32
            ).astype(BF16)

    to_up, to_down, to_across, to_sib = [None] * 2, [None] * 2, [None] * 2, [None] * 2
    for p in (0, 1):
        to_up[p] = copies.new(own(p), rows(z, h, p), up)
        to_down[1 - p] = copies.new(own(1 - p), rows(z, h, 1 - p), down)
        to_across[p] = copies.new(own(p), rows(z, h, p), across)
        to_sib[p] = copies.new(own(p), rows(z, h, p), sib)

    for load in loads:
        load.wait()
    for p in (0, 1):
        to_sib[p].wait_recv()
    project(z, h)

    to_up[0].wait_recv()
    c_up = forward(zm, h, 0, up)
    s_zm = [forward(zm, h, 0, sib), None]
    to_down[1].wait_recv()
    c_down = forward(zp, h, 1, down)
    s_zp = [None, forward(zp, h, 1, sib)]
    p_up, p_down, s_p = [None] * 2, [None] * 2, [None] * 2
    to_across[0].wait_recv()
    p_up[0] = forward(z, hh, 0, up)
    p_down[0] = forward(z, hh, 0, down)
    s_p[0] = forward(z, hh, 0, sib)
    to_up[1].wait_recv()
    s_zm[1] = forward(zm, h, 1, sib)
    to_down[0].wait_recv()
    s_zp[0] = forward(zp, h, 0, sib)
    to_across[1].wait_recv()
    p_up[1] = forward(z, hh, 1, up)
    p_down[1] = forward(z, hh, 1, down)
    s_p[1] = forward(z, hh, 1, sib)
    for p in (0, 1):
        s_zm[p].wait_recv()
    project(zm, h)
    c_up.wait_recv()
    c_y, s_c = [None] * 2, [None] * 2
    c_y[0] = forward(zz, h, 0, across)
    s_c[0] = forward(zz, h, 0, sib)
    c_down.wait_recv()
    c_y[1] = forward(zz, h, 1, across)
    s_c[1] = forward(zz, h, 1, sib)
    for p in (0, 1):
        s_zp[p].wait_recv()
    project(zp, h)
    for p in (0, 1):
        s_p[p].wait_recv()
    project(z, hh)
    s_pm, s_pp = [None] * 2, [None] * 2
    for p in (0, 1):
        p_up[p].wait_recv()
        s_pm[p] = forward(zm, hh, p, sib)
        p_down[p].wait_recv()
        s_pp[p] = forward(zp, hh, p, sib)
        if p == 0:
            for q in (0, 1):
                s_c[q].wait_recv()
            project(zz, h)
    for p in (0, 1):
        s_pm[p].wait_recv()
    project(zm, hh)
    s_cy = [None] * 2
    for p in (0, 1):
        c_y[p].wait_recv()
        s_cy[p] = forward(zz, hh, p, sib)
    for p in (0, 1):
        s_pp[p].wait_recv()
    project(zp, hh)
    for p in (0, 1):
        s_cy[p].wait_recv()
    project(zz, hh)
    copies.finish()


def gather_project(shard, wxz, wproj):
    return pl.pallas_call(
        gather_kernel,
        out_shape=jax.ShapeDtypeStruct((TOKENS, COLS), BF16),
        in_specs=[pl.BlockSpec(memory_space=pl.ANY)] * 3,
        out_specs=pl.BlockSpec(memory_space=pltpu.VMEM),
        scratch_shapes=[
            pltpu.VMEM((TOKENS, WIDTH), BF16),
            pltpu.VMEM((WIDTH, COLS), BF16),
            pltpu.SemaphoreType.DMA((30,)),
            pltpu.SemaphoreType.DMA((30,)),
            pltpu.SemaphoreType.DMA((5,)),
        ],
        compiler_params=pltpu.CompilerParams(
            collective_id=0, has_side_effects=True, vmem_limit_bytes=40 * MIB
        ),
        name="gather_project",
    )(shard, wxz, wproj)


def scan_kernel(proj, conv_w, conv_b, step_b, decay, skip, gain, out, squares, window, state):
    me = lax.axis_index("seq")
    group = me // 4
    x_at = pl.multiple_of(me * CHAN, CHAN)
    b_at = pl.multiple_of(4096 + (group // 2) * 128, 128)
    c_at = pl.multiple_of(4352 + (group // 2) * 128, 128)

    def own(ref):
        return jnp.concatenate(
            [ref[:, pl.ds(x_at, CHAN)], ref[:, pl.ds(b_at, 128)], ref[:, pl.ds(c_at, 128)]], axis=1
        )

    def iota(shape, dim):
        return lax.broadcasted_iota(jnp.int32, shape, dim)

    taps = own(conv_w)
    offset = own(conv_b)
    spread = (iota((128, CHAN), 0) == me * 8 + iota((128, CHAN), 1) // 32).astype(F32)

    def per_channel(ref):
        return jnp.dot(
            jnp.broadcast_to(ref[...], (8, 128)), spread, precision=HIGHEST, preferred_element_type=F32
        )[0:1]

    bias = per_channel(step_b)
    rate = -jnp.exp(per_channel(decay))
    direct = per_channel(skip)
    gains = gain[:, pl.ds(x_at, CHAN)]
    lower = iota((BLOCK, BLOCK), 0) >= iota((BLOCK, BLOCK), 1)
    lower_ones = lower.astype(F32)
    own_half = iota((BLOCK, 128), 1) // 64 == group % 2
    head_of = iota((BLOCK, CHAN), 1) // 32
    spread16 = spread.astype(BF16)

    window[0:8, :] = jnp.zeros((8, 512), F32)
    state[...] = jnp.zeros_like(state)

    def block(index, carry):
        at = pl.ds(pl.multiple_of(index * BLOCK, BLOCK), BLOCK)
        window[8 : 8 + BLOCK, :] = proj[at, pl.ds(256, 512)].astype(F32)
        conv = offset + taps[0:1] * window[5 : 5 + BLOCK, :]
        for k in range(1, 4):
            conv = conv + taps[k : k + 1] * window[5 + k : 5 + k + BLOCK, :]
        window[0:8, :] = window[BLOCK : BLOCK + 8, :]
        conv = (conv / (1.0 + jnp.exp(-conv))).astype(BF16)
        x = conv[:, :CHAN]
        b = conv[:, CHAN : CHAN + 128]
        c = jnp.where(own_half, conv[:, CHAN + 128 :], jnp.zeros((), BF16))
        step = jax.nn.softplus(
            jnp.dot(proj[at, pl.ds(768, 128)], spread16, preferred_element_type=F32) + bias
        )
        cumulus = jnp.dot(lower_ones, rate * step, precision=HIGHEST, preferred_element_type=F32)
        total = cumulus[BLOCK - 1 : BLOCK]
        cumulus_t = cumulus.T
        step_t = step.T
        scores = lax.dot_general(c, b, (((1,), (1,)), ((), ())), preferred_element_type=F32)
        mixing, values = [], []
        for head in range(8):
            lane = 32 * head
            gap = cumulus[:, lane : lane + 1] - cumulus_t[lane : lane + 1, :]
            gap = jnp.where(lower, gap, -1e30)
            mixing.append((scores * jnp.exp(gap) * step_t[lane : lane + 1, :]).astype(BF16))
            values.append(jnp.where(head_of == head, x, jnp.zeros((), BF16)))
        mixed = jnp.dot(
            jnp.concatenate(mixing, axis=1), jnp.concatenate(values, axis=0), preferred_element_type=F32
        )
        x32 = x.astype(F32)
        before = state[...]
        mixed = mixed + jnp.exp(cumulus) * jnp.dot(c, before.astype(BF16), preferred_element_type=F32)
        mixed = mixed + direct * x32
        weighted = (x32 * (jnp.exp(total - cumulus) * step)).astype(BF16)
        state[...] = jnp.exp(total) * before + lax.dot_general(
            b, weighted, (((0,), (0,)), ((), ())), preferred_element_type=F32
        )
        gate = proj[at, pl.ds(0, CHAN)].astype(F32)
        gated = mixed * (gate / (1.0 + jnp.exp(-gate)))
        squares[:, at] = lax.dot_general(
            jnp.ones((8, CHAN), F32),
            gated * gated,
            (((1,), (1,)), ((), ())),
            precision=HIGHEST,
            preferred_element_type=F32,
        )
        out[at, :] = (gated * gains).astype(BF16)
        return carry

    lax.fori_loop(0, TOKENS // BLOCK, block, 0)


def scan_gate(proj, conv_w, conv_b, step_b, decay, skip, gain):
    return pl.pallas_call(
        scan_kernel,
        out_shape=(
            jax.ShapeDtypeStruct((TOKENS, CHAN), BF16),
            jax.ShapeDtypeStruct((8, TOKENS), F32),
        ),
        in_specs=[pl.BlockSpec(memory_space=pltpu.VMEM)] * 7,
        out_specs=(pl.BlockSpec(memory_space=pltpu.VMEM),) * 2,
        scratch_shapes=[pltpu.VMEM((BLOCK + 8, 512), F32), pltpu.VMEM((128, CHAN), F32)],
        compiler_params=pltpu.CompilerParams(vmem_limit_bytes=40 * MIB),
        name="scan_gate",
    )(proj, conv_w, conv_b, step_b, decay, skip, gain)


def scatter_kernel(relay, gated, squares, wout, *refs):
    if relay:
        out, passed = refs[:2]
        refs = refs[2:]
    else:
        out = refs[0]
        refs = refs[1:]
    part, from_sib, got, stats, scale, staged, send_sem, recv_sem = refs
    sec, z, h, c = place()
    zp, zm, zz, hh = (z + 1) % 4, (z + 3) % 4, (z + 2) % 4, 1 - h

    def dev(z_, h_, c_):
        return (sec, z_ * 4 + h_ * 2 + c_)

    up, down, across, sib = dev(zp, h, c), dev(zm, h, c), dev(z, hh, c), dev(z, h, 1 - c)
    diag = dev(z, hh, 1 - c)
    here = z * 4 + h * 2 + c
    after, ahead = ((sec + 1) % 8, here), ((sec + 7) % 8, here)
    meet([up, down, across, sib, diag] + ([after, ahead] if relay else []))
    copies = Copies(send_sem, recv_sem)

    shares = [copies.new(squares, stats.at[i], t) for i, t in enumerate((sib, across, diag))]
    for share in shares:
        share.wait_recv()
    mean = (squares[...] + stats[0] + stats[1] + stats[2]) / 1024.0
    factor = lax.rsqrt(mean + 1e-05)
    for i in range(TOKENS // BLOCK):
        scale[pl.ds(i * BLOCK, BLOCK), :] = lax.dot_general(
            factor[:, i * BLOCK : (i + 1) * BLOCK],
            jnp.full((8, 128), 0.125, F32),
            (((0,), (0,)), ((), ())),
            precision=HIGHEST,
            preferred_element_type=F32,
        )

    def mine(z_, h_, p):
        start = pl.multiple_of((z_ * 2 + h_) * 128 + c * 64 + p * PIECE, PIECE)
        return part.at[pl.ds(start, PIECE)]

    def compute(z_, h_):
        start = pl.multiple_of((z_ * 2 + h_) * 128, 128)
        at = pl.ds(start, 128)
        rows_scale = jnp.concatenate([scale[at, :]] * 4, axis=1)
        lhs = gated[at, :]

        def tile(n, carry):
            cols = pl.ds(pl.multiple_of(n * 512, 512), 512)
            part[at, cols] = (
                jnp.dot(lhs, wout[:, cols], preferred_element_type=F32) * rows_scale
            ).astype(BF16)
            return carry

        lax.fori_loop(0, WIDTH // 512, tile, 0)
        src = part.at[pl.ds(pl.multiple_of(start + (1 - c) * 64, 64), 64)]
        dst = from_sib.at[pl.ds(pl.multiple_of((z_ * 2 + h_) * 64, 64), 64)]
        return copies.new(src, dst, sib)

    def add(dst, *others):
        def tile(n, carry):
            cols = pl.ds(pl.multiple_of(n * 512, 512), 512)
            total = dst[:, cols].astype(F32)
            for other in others:
                total = total + other[:, cols].astype(F32)
            dst[:, cols] = total.astype(BF16)
            return carry

        lax.fori_loop(0, WIDTH // 512, tile, 0)

    def paired(z_, h_, copy):
        copy.wait_recv()
        for p in (0, 1):
            start = pl.multiple_of((z_ * 2 + h_) * 64 + p * PIECE, PIECE)
            add(mine(z_, h_, p), from_sib.at[pl.ds(start, PIECE)])

    s0 = compute(zz, hh)
    s1 = compute(zp, hh)
    paired(zz, hh, s0)
    y1 = [copies.new(mine(zz, hh, p), got.at[p], across) for p in (0, 1)]
    s2 = compute(zm, hh)
    paired(zp, hh, s1)
    u5 = [copies.new(mine(zp, hh, p), got.at[2 + p], up) for p in (0, 1)]
    s3 = compute(zz, h)
    paired(zm, hh, s2)
    d5 = [copies.new(mine(zm, hh, p), got.at[4 + p], down) for p in (0, 1)]
    s4 = compute(zp, h)
    paired(zz, h, s3)
    s5 = compute(zm, h)
    paired(zp, h, s4)
    u4 = [copies.new(mine(zp, h, 0), got.at[6], up), None]
    s6 = compute(z, hh)
    paired(zm, h, s5)
    d4 = [None, copies.new(mine(zm, h, 1), got.at[9], down)]
    s7 = compute(z, h)
    paired(z, hh, s6)
    paired(z, h, s7)

    y1[0].wait_recv()
    add(mine(zz, h, 0), got.at[0])
    c_down = copies.new(mine(zz, h, 0), got.at[10], down)
    y1[1].wait_recv()
    add(mine(zz, h, 1), got.at[1])
    c_up = copies.new(mine(zz, h, 1), got.at[11], up)
    y6 = [None] * 2
    for p in (0, 1):
        u5[p].wait_recv()
        d5[p].wait_recv()
        add(mine(z, hh, p), got.at[2 + p], got.at[4 + p])
        y6[p] = copies.new(mine(z, hh, p), got.at[12 + p], across)
    c_down.wait_recv()
    add(mine(zm, h, 0), got.at[10])
    d4[0] = copies.new(mine(zm, h, 0), got.at[8], down)
    c_up.wait_recv()
    add(mine(zp, h, 1), got.at[11])
    u4[1] = copies.new(mine(zp, h, 1), got.at[7], up)

    relays = []
    for p in (0, 1):
        u4[p].wait_recv()
        d4[p].wait_recv()
        y6[p].wait_recv()
        own = mine(z, h, p)
        at = pl.ds(p * PIECE, PIECE)

        def tile(n, carry):
            cols = pl.ds(pl.multiple_of(n * 512, 512), 512)
            total = own[:, cols].astype(F32) + got[12 + p, :, cols].astype(F32)
            total = total + got[6 + p, :, cols].astype(F32) + got[8 + p, :, cols].astype(F32)
            out[at, cols] = total
            if relay:
                staged[at, cols] = total.astype(BF16)
            return carry

        lax.fori_loop(0, WIDTH // 512, tile, 0)
        if relay:
            relays.append(copies.new(staged.at[at], passed.at[at], after))
    for hop in relays:
        hop.wait_recv()
    copies.finish()


def project_scatter(relay, gated, squares, wout):
    shapes = [jax.ShapeDtypeStruct((64, WIDTH), F32)]
    if relay:
        shapes.append(jax.ShapeDtypeStruct((64, WIDTH), BF16))
    count = 3 + 8 + 14 + (2 if relay else 0)
    return pl.pallas_call(
        functools.partial(scatter_kernel, relay),
        out_shape=tuple(shapes),
        in_specs=[pl.BlockSpec(memory_space=pltpu.VMEM)] * 3,
        out_specs=(pl.BlockSpec(memory_space=pltpu.VMEM),) * len(shapes),
        scratch_shapes=[
            pltpu.VMEM((TOKENS, WIDTH), BF16),
            pltpu.VMEM((TOKENS // 2, WIDTH), BF16),
            pltpu.VMEM((14, PIECE, WIDTH), BF16),
            pltpu.VMEM((3, 8, TOKENS), F32),
            pltpu.VMEM((TOKENS, 128), F32),
            pltpu.VMEM((64, WIDTH), BF16),
            pltpu.SemaphoreType.DMA((count,)),
            pltpu.SemaphoreType.DMA((count,)),
        ],
        compiler_params=pltpu.CompilerParams(
            collective_id=1 if relay else 2, has_side_effects=True, vmem_limit_bytes=48 * MIB
        ),
        name="project_scatter",
    )(gated, squares, wout)


def on_device(
    inflow,
    fresh,
    proj_weight,
    xz_weight,
    conv_weight,
    conv_bias,
    step_bias,
    decay_log,
    skip_weight,
    norm_gain,
    out_weight,
):
    wxz = xz_weight[0].reshape(WIDTH, 2 * CHAN)
    wproj = proj_weight[0]

    def mixer(shard):
        proj = gather_project(shard, wxz, wproj)
        return scan_gate(
            proj, conv_weight[0], conv_bias, step_bias, decay_log, skip_weight, norm_gain
        )

    first, passed = project_scatter(True, *mixer(inflow[0]), out_weight[0])
    entering = jnp.where(lax.axis_index("section") == 0, fresh[0], passed)
    (second,) = project_scatter(False, *mixer(entering), out_weight[0])
    return jnp.stack([first, second])[None]


def solution(mesh):
    placed = (
        P("section", "seq", None),
        P(None, "seq", None),
        P("section", None, None),
        P("section", None, None, "seq"),
        P("section", None, None),
        P("section", None),
        P("section", None),
        P("section", None),
        P("section", None),
        P("section", None),
        P("section", "seq", None),
    )
    return jax.shard_map(
        on_device,
        mesh=mesh,
        in_specs=placed,
        out_specs=P("section", None, "seq", None),
        check_vma=False,
    )
```

time: 825 us -> 217 us (0.26)
  waiting for transfers between devices: 433 us -> 0 us
  Pallas kernels: 0 us -> 208 us
  blocking collectives: 133 us -> 0 us
  matrix products: 107 us -> 0 us
  local copies, waits for them, and re-layouts: 109 us -> 3.89 us
  other arithmetic: 21.6 us -> 1.58 us
  between operations: 13.6 us -> 0.14 us
    reduce_scatter x2 -> x0, waiting for transfers between devices: 286 us -> none  [layer(): lax.psum_scatter(jnp.dot(normed, out_local, preferred_element_type=jnp.fl...]
    pallas_call x0 -> x6, Pallas kernels: none -> 208 us  [the longest x2 104 us: project_scatter(): pl.pallas_call(functools.partial(scatter_kernel, relay), out_shape=tuple(...]
    psum x2 -> x0, blocking collectives: 133 us -> none  [layer(): summed_squares = lax.psum(group_mask * own_squares[None, :], 'seq')]
    all_gather x2 -> x0, waiting for transfers between devices: 132 us -> none  [layer(): lax.all_gather(shard, 'seq', axis=0, tiled=True)]
    dot_general x68 -> x0, matrix products: 107 us -> none  [the longest x2 23.6 us: layer(): jnp.dot(lax.all_gather(shard, 'seq', axis=0, tiled=True), own_weight, pre...]
    dynamic_update_slice x16 -> x0, local copies, waits for them, and re-layouts: 71.3 us -> none  [layer(): lax.scan(run_block, start_state, (x_blocks, b_blocks, c_blocks, step_bloc...]
    dynamic_slice x55 -> x0, local copies, waits for them, and re-layouts: 23.7 us -> none  [the longest x48 14.3 us: layer(): lax.scan(run_block, start_state, (x_blocks, b_blocks, c_blocks, step_bloc...]
    ppermute x1 -> x0, waiting for transfers between devices: 14 us -> none  [shifted(): lax.ppermute(value, axis, [(source, source + steps) for source in range(l...]
  transfers between devices with their start and end apart: 5 -> 0, of which waited for: 5 -> 0; matrix products, arithmetic and copies ran while one was open for 2% -> 0% of each run, Pallas kernels for 0% -> 0%
where the time goes in v1:
time: 217 us; the launch traced here: 214 us
  Pallas kernels  208 us (96%)
  local copies, waits for them, and re-layouts  3.89 us (2%)
    pallas_call x2, Pallas kernels, project_scatter(): pl.pallas_call(functools.partial(scatter_kernel, relay), out_shape=tuple(...  104 us
    pallas_call x2, Pallas kernels, gather_project(): pl.pallas_call(gather_kernel, out_shape=jax.ShapeDtypeStruct((TOKENS, COL...  81.4 us
    pallas_call x2, Pallas kernels, scan_gate(): pl.pallas_call(scan_kernel, out_shape=(jax.ShapeDtypeStruct((TOKENS, CHAN...  22.6 us

profile of v1, /device:TPU:14, one launch (start us, length us, event | category | flops | bytes accessed | tf_op | source)
XLA Modules:
  0.0 213.8 jit_solution(5994360235304192652)
XLA Ops:
  0.0 0.0 copy-start
  0.0 3.1 %copy.12 = bf16[512,8,2,256]{3,1,2,0:T(8,128)(2,1)S(1)} copy(bf16[512,8,2,256]{3,2,1,0:T(2,128)(2,1)} %bitcast.24) | data formatting | bytes 8388608
  3.1 0.6 copy-done
  3.7 0.1 copy-done.2
  3.9 0.0 copy-start.7
  3.9 0.0 copy-start.8
  3.9 0.0 copy-start.1
  3.9 41.9 %gather_project.2.proj = bf16[1024,896]{1,0:T(8,128)(2,1)S(1)} custom-call(bf16[64,4096]{1,0:T(8,128)(2,1)S(1)} %bitcast.21, bf16[4096,512]{1,0:T(8,128)(2,1)S(1)} %bitcast.13, bf16[4096,640]{1,0:T(8,128)(2,1)S(1)} %bitcast.15), custom_call_target="tpu_custom_call" | custom-call | tf_op jit(solution)/shard_map/gather_project/pallas_call | solution.py:178
  45.8 0.0 copy-done.3
  45.8 0.0 copy-done.4
  45.8 0.0 copy-done.5
  45.9 0.0 copy-done.6
  45.9 0.0 copy-done.7
  45.9 0.0 copy-done.8
  45.9 0.0 copy-start.9
  45.9 11.3 %scan_gate.2 = (bf16[1024,256]{1,0:T(8,128)(2,1)S(1)}, f32[8,1024]{1,0:T(8,128)S(1)}) custom-call(bf16[1024,896]{1,0:T(8,128)(2,1)S(1)} %gather_project.2.proj, f32[4,4608]{1,0:T(4,128)S(1)} %bitcast.22, f32[1,4608]{1,0:T(1,128)S(1)} %copy-done.4, f32[1,128]{1,0:T(1,128)S(1)} %copy-done.6, f32[1,128]{1,0:T(1,128)S(1)} %copy-done.7, f32[1,128]{1,0:T(1,128)S(1)} %copy-done.8, ...), custom_call_target="tpu_custom_call" | custom-call | tf_op jit(solution)/shard_map/scan_gate/pallas_call | solution.py:287
  57.2 0.0 copy-done.1
  57.2 57.0 %project_scatter.2 = (f32[64,4096]{1,0:T(8,128)S(1)}, bf16[64,4096]{1,0:T(8,128)(2,1)S(1)}) custom-call(bf16[1024,256]{1,0:T(8,128)(2,1)S(1)} %get-tuple-element.11.gated, f32[8,1024]{1,0:T(8,128)S(1)} %get-tuple-element.12.squares, bf16[256,4096]{1,0:T(8,128)(2,1)S(1)} %bitcast.17), custom_call_target="tpu_custom_call" | custom-call | tf_op jit(solution)/shard_map/project_scatter/pallas_call | solution.py:446
  114.2 0.0 copy-done.9
  114.2 0.1 bitcast_select_fusion.shard
  114.3 39.5 %gather_project.3.proj = bf16[1024,896]{1,0:T(8,128)(2,1)S(1)} custom-call(bf16[64,4096]{1,0:T(8,128)(2,1)S(1)} %bitcast_select_fusion.shard, bf16[4096,512]{1,0:T(8,128)(2,1)S(1)} %bitcast.14, bf16[4096,640]{1,0:T(8,128)(2,1)S(1)} %bitcast.16), custom_call_target="tpu_custom_call" | custom-call | tf_op jit(solution)/shard_map/gather_project/pallas_call | solution.py:178
  153.8 11.3 %scan_gate.3 = (bf16[1024,256]{1,0:T(8,128)(2,1)S(1)}, f32[8,1024]{1,0:T(8,128)S(1)}) custom-call(bf16[1024,896]{1,0:T(8,128)(2,1)S(1)} %gather_project.3.proj, f32[4,4608]{1,0:T(4,128)S(1)} %bitcast.23, f32[1,4608]{1,0:T(1,128)S(1)} %copy-done.4, f32[1,128]{1,0:T(1,128)S(1)} %copy-done.6, f32[1,128]{1,0:T(1,128)S(1)} %copy-done.7, f32[1,128]{1,0:T(1,128)S(1)} %copy-done.8, ...), custom_call_target="tpu_custom_call" | custom-call | tf_op jit(solution)/shard_map/scan_gate/pallas_call | solution.py:287
  165.1 47.2 %project_scatter.3 = f32[64,4096]{1,0:T(8,128)S(1)} custom-call(bf16[1024,256]{1,0:T(8,128)(2,1)S(1)} %get-tuple-element.15.gated, f32[8,1024]{1,0:T(8,128)S(1)} %get-tuple-element.16.squares, bf16[256,4096]{1,0:T(8,128)(2,1)S(1)} %bitcast.18), custom_call_target="tpu_custom_call" | custom-call | tf_op jit(solution)/shard_map/project_scatter/pallas_call | solution.py:446
  212.3 1.5 maximum_bitcast_fusion
  (5 shorter events, 0.0 us)
Async XLA Ops:
  0.0 3.7 %copy-start = (bf16[1,4096,640]{2,1,0:T(8,128)(2,1)S(1)}, bf16[1,4096,640]{2,1,0:T(8,128)(2,1)}, u32[]{:S(2)}) copy-start(bf16[1,4096,640]{2,1,0:T(8,128)(2,1)} %param.13) | copy-start | bytes 15728644
  0.0 3.9 %copy-start.2 = (bf16[1,64,4096]{2,1,0:T(8,128)(2,1)S(1)}, bf16[1,64,4096]{2,1,0:T(8,128)(2,1)}, u32[]{:S(2)}) copy-start(bf16[1,64,4096]{2,1,0:T(8,128)(2,1)} %param.11) | copy-start | bytes 1572868
  3.9 42.0 %copy-start.3 = (f32[1,4,4608]{2,1,0:T(4,128)S(1)}, f32[1,4,4608]{2,1,0:T(4,128)}, u32[]{:S(2)}) copy-start(f32[1,4,4608]{2,1,0:T(4,128)} %param.15) | copy-start | bytes 221188
  3.9 42.0 %copy-start.4 = (f32[1,4608]{1,0:T(1,128)S(1)}, f32[1,4608]{1,0:T(1,128)}, u32[]{:S(2)}) copy-start(f32[1,4608]{1,0:T(1,128)} %conv_b.3) | copy-start | bytes 55300
  3.9 42.0 %copy-start.5 = (f32[1,4096]{1,0:T(1,128)S(1)}, f32[1,4096]{1,0:T(1,128)}, u32[]{:S(2)}) copy-start(f32[1,4096]{1,0:T(1,128)} %gain.3) | copy-start | bytes 49156
  3.9 42.0 %copy-start.6 = (f32[1,128]{1,0:T(1,128)S(1)}, f32[1,128]{1,0:T(1,128)}, u32[]{:S(2)}) copy-start(f32[1,128]{1,0:T(1,128)} %step_b.3) | copy-start | bytes 1540
  3.9 42.0 %copy-start.7 = (f32[1,128]{1,0:T(1,128)S(1)}, f32[1,128]{1,0:T(1,128)}, u32[]{:S(2)}) copy-start(f32[1,128]{1,0:T(1,128)} %decay.3) | copy-start | bytes 1540
  3.9 42.0 %copy-start.8 = (f32[1,128]{1,0:T(1,128)S(1)}, f32[1,128]{1,0:T(1,128)}, u32[]{:S(2)}) copy-start(f32[1,128]{1,0:T(1,128)} %skip.3) | copy-start | bytes 1540
  3.9 53.3 %copy-start.1 = (bf16[1,256,4096]{2,1,0:T(8,128)(2,1)S(1)}, bf16[1,256,4096]{2,1,0:T(8,128)(2,1)}, u32[]{:S(2)}) copy-start(bf16[1,256,4096]{2,1,0:T(8,128)(2,1)} %param.21) | copy-start | bytes 6291460
  45.9 68.3 %copy-start.9 = (bf16[1,64,4096]{2,1,0:T(8,128)(2,1)S(1)}, bf16[1,64,4096]{2,1,0:T(8,128)(2,1)}, u32[]{:S(2)}) copy-start(bf16[1,64,4096]{2,1,0:T(8,128)(2,1)} %param.12) | copy-start | bytes 1572868

commit v2 on v0

v2 whole, which is shorter than its diff:
```python
import functools

import jax
import jax.numpy as jnp
from jax import lax
from jax.experimental import pallas as pl
from jax.experimental.pallas import tpu as pltpu
from jax.sharding import PartitionSpec as P

MESH = pl.DeviceIdType.MESH
F32 = jnp.float32
BF16 = jnp.bfloat16
HIGHEST = lax.Precision.HIGHEST
TOKENS = 1024
WIDTH = 4096
CHAN = 256
BLOCK = 128
BLOCKS = TOKENS // BLOCK
ROWS = 64
HALF = WIDTH // 2
COLS = 896
TILES = ((0, 256), (256, 256), (512, 256), (768, 128))
LAST = 7
COPIES = 192
MIB = 2**20


def aligned(value, by):
    return pl.multiple_of(value, by)


def iota(shape, dim):
    return lax.broadcasted_iota(jnp.int32, shape, dim)


def columns(p):
    return pl.ds(p * HALF, HALF)


class Place:
    def __init__(self):
        self.sec = lax.axis_index("section")
        self.me = lax.axis_index("seq")
        self.z, self.h, self.c = self.me // 4, (self.me // 2) % 2, self.me % 2
        self.zp, self.zm, self.zz = (self.z + 1) % 4, (self.z + 3) % 4, (self.z + 2) % 4
        self.hh = 1 - self.h
        self.up = self.device(self.zp, self.h, self.c)
        self.down = self.device(self.zm, self.h, self.c)
        self.across = self.device(self.z, self.hh, self.c)
        self.sib = self.device(self.z, self.h, 1 - self.c)
        self.diag = self.device(self.z, self.hh, 1 - self.c)
        self.after = ((self.sec + 1) % 8, self.me)
        self.ahead = ((self.sec + 7) % 8, self.me)

    def device(self, z, h, c):
        return (self.sec, z * 4 + h * 2 + c)

    def meet(self):
        targets = [self.up, self.down, self.across, self.sib, self.diag, self.after, self.ahead]
        barrier = pltpu.get_barrier_semaphore()
        for target in targets:
            pl.semaphore_signal(barrier, inc=1, device_id=target, device_id_type=MESH)
        pl.semaphore_wait(barrier, len(targets))


class Copies:
    def __init__(self, send_sem, recv_sem):
        self.send_sem, self.recv_sem = send_sem, recv_sem
        self.count = 0
        self.open = []

    def make(self, src, dst, target):
        index = self.count
        self.count += 1
        return pltpu.make_async_remote_copy(
            src_ref=src,
            dst_ref=dst,
            send_sem=self.send_sem.at[index],
            recv_sem=self.recv_sem.at[index],
            device_id=target,
            device_id_type=MESH,
        )

    def new(self, src, dst, target):
        copy = self.make(src, dst, target)
        copy.start()
        self.open.append(copy)
        return copy

    def finish(self):
        for copy in self.open:
            copy.wait_send()
        self.open = []


class Gather:
    def __init__(self, at, copies, source, act, weight, acc, proj):
        self.at, self.copies, self.source = at, copies, source
        self.act, self.weight, self.acc, self.proj = act, weight, acc, proj
        self.got = {}

    def rows(self, z, h, p, half=None):
        start = (z * 2 + h) * 128 + self.at.c * ROWS
        if half is None:
            return self.act.at[pl.ds(aligned(start, ROWS), ROWS), columns(p)]
        return self.act.at[pl.ds(aligned(start + half * 32, 32), 32), columns(p)]

    def forward(self, z, h, p, target, half=None):
        return self.copies.new(self.rows(z, h, p, half), self.rows(z, h, p, half), target)

    def share(self, name, z, h, p, half=None):
        self.got.setdefault((name, p), []).append(self.forward(z, h, p, self.at.sib, half))

    def own(self, p):
        at = self.at
        src = self.source.at[:, columns(p)]
        dst = self.rows(at.z, at.h, p)
        for name, target in (("up", at.up), ("down", at.down), ("across", at.across), ("own", at.sib)):
            self.got[name, p] = [self.copies.new(src, dst, target)]

    def arrived(self, name, p):
        for copy in self.got[name, p]:
            copy.wait_recv()

    def near(self, p):
        at = self.at
        self.arrived("up", p)
        self.got["cu", p] = [self.forward(at.zm, at.h, p, at.up, 0)]
        self.arrived("down", p)
        self.got["cd", p] = [self.forward(at.zp, at.h, p, at.down, 1)]
        self.share("s_zm", at.zm, at.h, p)
        self.share("s_zp", at.zp, at.h, p)
        self.arrived("across", p)
        self.got["pu", p] = [self.forward(at.z, at.hh, p, at.up)]
        self.got["pd", p] = [self.forward(at.z, at.hh, p, at.down)]
        self.share("s_p", at.z, at.hh, p)

    def far(self, p):
        at = self.at
        for name, half in (("cu", 0), ("cd", 1)):
            self.arrived(name, p)
            self.got["cy%d" % half, p] = [self.forward(at.zz, at.h, p, at.across, half)]
            self.share("s_c", at.zz, at.h, p, half)

    def beside(self, p):
        at = self.at
        self.arrived("pu", p)
        self.share("s_pm", at.zm, at.hh, p)
        self.arrived("pd", p)
        self.share("s_pp", at.zp, at.hh, p)

    def last(self, p):
        at = self.at
        for half in (0, 1):
            self.arrived("cy%d" % half, p)
            self.share("s_cy", at.zz, at.hh, p, half)

    def project(self, name, z, h, p):
        self.arrived(name, p)
        at = pl.ds(aligned((z * 2 + h) * 128, 128), 128)
        for first, size in TILES:
            cols = pl.ds(first, size)
            part = jnp.dot(
                self.act[at, columns(p)], self.weight[columns(p), cols], preferred_element_type=F32
            )
            if p == 0:
                self.acc[at, cols] = part
            else:
                self.proj[at, cols] = (self.acc[at, cols] + part).astype(BF16)

    def project_near(self, p):
        at = self.at
        self.project("own", at.z, at.h, p)
        self.project("s_zm", at.zm, at.h, p)
        self.project("s_zp", at.zp, at.h, p)
        self.project("s_p", at.z, at.hh, p)

    def project_beside(self, p):
        at = self.at
        self.project("s_pm", at.zm, at.hh, p)
        self.project("s_pp", at.zp, at.hh, p)

    def rest(self):
        at = self.at
        self.project_near(0)
        self.near(1)
        self.far(0)
        self.project_near(1)
        self.beside(0)
        self.project("s_c", at.zz, at.h, 0)
        self.far(1)
        self.project_beside(0)
        self.last(0)
        self.project("s_c", at.zz, at.h, 1)
        self.beside(1)
        self.project("s_cy", at.zz, at.hh, 0)
        self.project_beside(1)
        self.last(1)
        self.project("s_cy", at.zz, at.hh, 1)


class Mixer:
    def __init__(self, at, params, proj, conved, steps, sums, entering, window, gated, squares):
        self.proj, self.conved, self.steps, self.sums = proj, conved, steps, sums
        self.entering, self.window, self.gated, self.squares = entering, window, gated, squares
        conv_w, conv_b, step_b, decay, skip, gain = params
        group = at.me // 4
        x_at = aligned(at.me * CHAN, CHAN)
        b_at = aligned(4096 + (group // 2) * 128, 128)
        c_at = aligned(4352 + (group // 2) * 128, 128)

        def own(ref):
            return jnp.concatenate(
                [ref[:, pl.ds(x_at, CHAN)], ref[:, pl.ds(b_at, 128)], ref[:, pl.ds(c_at, 128)]], axis=1
            )

        spread = (iota((128, CHAN), 0) == at.me * 8 + iota((128, CHAN), 1) // 32).astype(F32)

        def per_channel(ref):
            wide = jnp.broadcast_to(ref[...], (8, 128))
            return jnp.dot(wide, spread, precision=HIGHEST, preferred_element_type=F32)[0:1]

        self.taps, self.offset = own(conv_w), own(conv_b)
        self.bias = per_channel(step_b)
        self.rate = -jnp.exp(per_channel(decay))
        self.direct = per_channel(skip)
        self.gains = gain[:, pl.ds(x_at, CHAN)]
        self.spread = spread.astype(BF16)
        self.half = group % 2

    def states(self):
        taps, window = self.taps, self.window
        lower_ones = (iota((BLOCK, BLOCK), 0) >= iota((BLOCK, BLOCK), 1)).astype(F32)
        own_half = iota((BLOCK, 128), 1) // 64 == self.half
        window[0:8, :] = jnp.zeros((8, 512), F32)

        def block(index, before):
            at = pl.ds(aligned(index * BLOCK, BLOCK), BLOCK)
            window[8 : 8 + BLOCK, :] = self.proj[at, pl.ds(256, 512)].astype(F32)
            conv = self.offset + taps[0:1] * window[5 : 5 + BLOCK, :]
            for k in range(1, 4):
                conv = conv + taps[k : k + 1] * window[5 + k : 5 + k + BLOCK, :]
            window[0:8, :] = window[BLOCK : BLOCK + 8, :]
            conv = (conv / (1.0 + jnp.exp(-conv))).astype(BF16)
            x = conv[:, :CHAN]
            b = conv[:, CHAN : CHAN + 128]
            c = jnp.where(own_half, conv[:, CHAN + 128 :], jnp.zeros((), BF16))
            self.conved[at, pl.ds(0, CHAN)] = x
            self.conved[at, pl.ds(CHAN, 128)] = b
            self.conved[at, pl.ds(CHAN + 128, 128)] = c
            step = jax.nn.softplus(
                jnp.dot(self.proj[at, pl.ds(768, 128)], self.spread, preferred_element_type=F32)
                + self.bias
            )
            cumulus = jnp.dot(
                lower_ones, self.rate * step, precision=HIGHEST, preferred_element_type=F32
            )
            total = cumulus[BLOCK - 1 : BLOCK]
            self.steps[at, :] = step
            self.sums[at, :] = cumulus
            self.entering[at, :] = before.astype(BF16)
            weighted = (x.astype(F32) * (jnp.exp(total - cumulus) * step)).astype(BF16)
            return jnp.exp(total) * before + lax.dot_general(
                b, weighted, (((0,), (0,)), ((), ())), preferred_element_type=F32
            )

        lax.fori_loop(0, BLOCKS, block, jnp.zeros((128, CHAN), F32))

    def outputs(self, z):
        lower = iota((BLOCK, BLOCK), 0) >= iota((BLOCK, BLOCK), 1)
        head_of = iota((BLOCK, CHAN), 1) // 32

        def block(index, carry):
            at = pl.ds(aligned(z * 256 + index * BLOCK, BLOCK), BLOCK)
            x = self.conved[at, pl.ds(0, CHAN)]
            b = self.conved[at, pl.ds(CHAN, 128)]
            c = self.conved[at, pl.ds(CHAN + 128, 128)]
            cumulus = self.sums[at, :]
            cumulus_t = cumulus.T
            step_t = self.steps[at, :].T
            scores = lax.dot_general(c, b, (((1,), (1,)), ((), ())), preferred_element_type=F32)
            mixing, values = [], []
            for head in range(8):
                lane = 32 * head
                gap = cumulus[:, lane : lane + 1] - cumulus_t[lane : lane + 1, :]
                gap = jnp.where(lower, gap, -1e30)
                mixing.append((scores * jnp.exp(gap) * step_t[lane : lane + 1, :]).astype(BF16))
                values.append(jnp.where(head_of == head, x, jnp.zeros((), BF16)))
            mixed = jnp.dot(
                jnp.concatenate(mixing, axis=1),
                jnp.concatenate(values, axis=0),
                preferred_element_type=F32,
            )
            mixed = mixed + jnp.exp(cumulus) * jnp.dot(
                c, self.entering[at, :], preferred_element_type=F32
            )
            mixed = mixed + self.direct * x.astype(F32)
            gate = self.proj[at, pl.ds(0, CHAN)].astype(F32)
            gated = mixed * (gate / (1.0 + jnp.exp(-gate)))
            self.squares[:, at] = lax.dot_general(
                jnp.ones((8, CHAN), F32),
                gated * gated,
                (((1,), (1,)), ((), ())),
                precision=HIGHEST,
                preferred_element_type=F32,
            )
            self.gated[at, :] = (gated * self.gains).astype(BF16)
            return carry

        lax.fori_loop(0, 2, block, 0)


class Scatter:
    def __init__(self, at, copies, mixer, wout, part, from_sib, got, stats, scale):
        self.at, self.copies, self.mixer, self.wout = at, copies, mixer, wout
        self.part, self.from_sib, self.got, self.stats, self.scale = part, from_sib, got, stats, scale
        self.sent = {}

    def gate(self, z):
        self.mixer.outputs(z)
        cols = pl.ds(aligned(z * 256, 256), 256)
        squares = self.mixer.squares.at[:, cols]
        self.shares = [
            self.copies.new(squares, self.stats.at[i, :, cols], target)
            for i, target in enumerate((self.at.sib, self.at.across, self.at.diag))
        ]
        return z, self.shares

    def factor(self, gate):
        z, shares = gate
        for share in shares:
            share.wait_recv()
        for i in (0, 1):
            at = pl.ds(aligned(z * 256 + i * 128, 128), 128)
            total = self.mixer.squares[:, at] + self.stats[0, :, at]
            total = total + self.stats[1, :, at] + self.stats[2, :, at]
            self.scale[at, :] = lax.dot_general(
                lax.rsqrt(total / 1024.0 + 1e-05),
                jnp.full((8, 128), 0.125, F32),
                (((0,), (0,)), ((), ())),
                precision=HIGHEST,
                preferred_element_type=F32,
            )

    def mine(self, z, h, p, half=None):
        start = (z * 2 + h) * 128 + self.at.c * ROWS
        if half is None:
            return self.part.at[pl.ds(aligned(start, ROWS), ROWS), columns(p)]
        return self.part.at[pl.ds(aligned(start + half * 32, 32), 32), columns(p)]

    def compute(self, z, h, p):
        start = aligned((z * 2 + h) * 128, 128)
        at = pl.ds(start, 128)
        lhs = self.mixer.gated[at, :]

        def tile(n, carry):
            cols = pl.ds(aligned(p * HALF + n * 512, 512), 512)
            self.part[at, cols] = jnp.dot(
                lhs, self.wout[:, cols], preferred_element_type=F32
            ).astype(BF16)
            return carry

        lax.fori_loop(0, HALF // 512, tile, 0)
        src = self.part.at[pl.ds(aligned(start + (1 - self.at.c) * ROWS, ROWS), ROWS), columns(p)]
        dst = self.from_sib.at[pl.ds(aligned((z * 2 + h) * ROWS, ROWS), ROWS), columns(p)]
        return self.copies.new(src, dst, self.at.sib)

    def pair(self, z, h, p, copy):
        copy.wait_recv()
        own = self.mine(z, h, p)
        other = self.from_sib.at[pl.ds(aligned((z * 2 + h) * ROWS, ROWS), ROWS), columns(p)]
        rows = pl.ds(aligned((z * 2 + h) * 128 + self.at.c * ROWS, ROWS), ROWS)
        scale = jnp.concatenate([self.scale[rows, :]] * 2, axis=1)

        def tile(n, carry):
            cols = pl.ds(aligned(n * 256, 256), 256)
            total = own[:, cols].astype(F32) + other[:, cols].astype(F32)
            own[:, cols] = (total * scale).astype(BF16)
            return carry

        lax.fori_loop(0, HALF // 256, tile, 0)

    @staticmethod
    def add(dst, *others):
        def tile(n, carry):
            cols = pl.ds(aligned(n * 256, 256), 256)
            total = dst[:, cols].astype(F32)
            for other in others:
                total = total + other[:, cols].astype(F32)
            dst[:, cols] = total.astype(BF16)
            return carry

        lax.fori_loop(0, HALF // 256, tile, 0)

    def send(self, name, src, slot, p, target, half=None):
        dst = self.got.at[p, slot]
        if half is not None:
            dst = self.got.at[p, slot, pl.ds(half * 32, 32)]
        self.sent.setdefault((name, p), []).append(self.copies.new(src, dst, target))

    def arrived(self, name, p):
        for copy in self.sent[name, p]:
            copy.wait_recv()

    def first(self):
        at = self.at
        g_zz = self.gate(at.zz)
        c_zzhh = self.compute(at.zz, at.hh, 0)
        g_zp = self.gate(at.zp)
        self.factor(g_zz)
        self.pair(at.zz, at.hh, 0, c_zzhh)
        self.send("y1", self.mine(at.zz, at.hh, 0), 0, 0, at.across)
        c_zphh = self.compute(at.zp, at.hh, 0)
        g_zm = self.gate(at.zm)
        self.factor(g_zp)
        self.pair(at.zp, at.hh, 0, c_zphh)
        self.send("u5", self.mine(at.zp, at.hh, 0), 1, 0, at.up)
        c_zmhh = self.compute(at.zm, at.hh, 0)
        c_zzh = self.compute(at.zz, at.h, 0)
        c_zph = self.compute(at.zp, at.h, 0)
        self.factor(g_zm)
        self.pair(at.zm, at.hh, 0, c_zmhh)
        self.send("d5", self.mine(at.zm, at.hh, 0), 2, 0, at.down)
        self.pair(at.zz, at.h, 0, c_zzh)
        self.pair(at.zp, at.h, 0, c_zph)
        self.send("u4", self.mine(at.zp, at.h, 0, 0), 3, 0, at.up, 0)
        c_zmh = self.compute(at.zm, at.h, 0)
        g_z = self.gate(at.z)
        self.pair(at.zm, at.h, 0, c_zmh)
        self.send("d4", self.mine(at.zm, at.h, 0, 1), 4, 0, at.down, 1)
        c_zhh = self.compute(at.z, at.hh, 0)
        c_zh = self.compute(at.z, at.h, 0)
        self.factor(g_z)
        self.pair(at.z, at.hh, 0, c_zhh)
        self.pair(at.z, at.h, 0, c_zh)

    def second(self):
        at = self.at
        c_zzhh = self.compute(at.zz, at.hh, 1)
        c_zphh = self.compute(at.zp, at.hh, 1)
        c_zmhh = self.compute(at.zm, at.hh, 1)
        self.cross(0)
        self.pair(at.zz, at.hh, 1, c_zzhh)
        self.send("y1", self.mine(at.zz, at.hh, 1), 0, 1, at.across)
        self.pair(at.zp, at.hh, 1, c_zphh)
        self.send("u5", self.mine(at.zp, at.hh, 1), 1, 1, at.up)
        self.pair(at.zm, at.hh, 1, c_zmhh)
        self.send("d5", self.mine(at.zm, at.hh, 1), 2, 1, at.down)
        self.side(0)
        c_zzh = self.compute(at.zz, at.h, 1)
        c_zph = self.compute(at.zp, at.h, 1)
        c_zmh = self.compute(at.zm, at.h, 1)
        self.pair(at.zz, at.h, 1, c_zzh)
        self.join(0)
        self.pair(at.zp, at.h, 1, c_zph)
        self.send("u4", self.mine(at.zp, at.h, 1, 0), 3, 1, at.up, 0)
        self.pair(at.zm, at.h, 1, c_zmh)
        self.send("d4", self.mine(at.zm, at.h, 1, 1), 4, 1, at.down, 1)
        c_zhh = self.compute(at.z, at.hh, 1)
        c_zh = self.compute(at.z, at.h, 1)
        self.pair(at.z, at.hh, 1, c_zhh)
        self.pair(at.z, at.h, 1, c_zh)

    def cross(self, p):
        at = self.at
        self.arrived("y1", p)
        self.add(self.mine(at.zz, at.h, p), self.got.at[p, 0])
        self.send("c_down", self.mine(at.zz, at.h, p, 0), 5, p, at.down, 0)
        self.send("c_up", self.mine(at.zz, at.h, p, 1), 5, p, at.up, 1)

    def side(self, p):
        at = self.at
        self.arrived("u5", p)
        self.arrived("d5", p)
        self.add(self.mine(at.z, at.hh, p), self.got.at[p, 1], self.got.at[p, 2])
        self.send("y6", self.mine(at.z, at.hh, p), 6, p, at.across)

    def join(self, p):
        at = self.at
        self.arrived("c_down", p)
        self.add(self.mine(at.zm, at.h, p, 0), self.got.at[p, 5, pl.ds(0, 32)])
        self.send("d4", self.mine(at.zm, at.h, p, 0), 4, p, at.down, 0)
        self.arrived("c_up", p)
        self.add(self.mine(at.zp, at.h, p, 1), self.got.at[p, 5, pl.ds(32, 32)])
        self.send("u4", self.mine(at.zp, at.h, p, 1), 3, p, at.up, 1)

    def total(self, p, out, staged):
        at = self.at
        for name in ("y6", "u4", "d4"):
            self.arrived(name, p)
        own = self.mine(at.z, at.h, p)

        def tile(n, carry):
            cols = pl.ds(aligned(n * 256, 256), 256)
            wide = pl.ds(aligned(p * HALF + n * 256, 256), 256)
            total = own[:, cols].astype(F32) + self.got[p, 6, :, cols].astype(F32)
            total = total + self.got[p, 3, :, cols].astype(F32) + self.got[p, 4, :, cols].astype(F32)
            out[:, wide] = total
            if staged is not None:
                staged[:, wide] = total.astype(BF16)
            return carry

        lax.fori_loop(0, HALF // 256, tile, 0)


def kernel(
    inflow, fresh, wxz, wproj, wout, conv_w, conv_b, step_b, decay, skip, gain, out,
    act, weight, acc, proj, conved, steps, sums, entering, window, gated, squares,
    part, from_sib, got, stats, scale, staged, received, send_sem, recv_sem, local_sem,
):
    at = Place()
    pair = at.z // 2
    here = pl.ds(aligned(at.me * ROWS, ROWS), ROWS)
    loads = []
    for index, (src, dst) in enumerate(
        [
            (inflow, act.at[here]),
            (wxz, weight.at[:, pl.ds(0, 2 * CHAN)]),
            (wproj.at[:, pl.ds(aligned(pair * 128, 128), 128)], weight.at[:, pl.ds(512, 128)]),
            (wproj.at[:, pl.ds(aligned(256 + pair * 128, 128), 128)], weight.at[:, pl.ds(640, 128)]),
            (wproj.at[:, pl.ds(512, 128)], weight.at[:, pl.ds(768, 128)]),
        ]
    ):
        load = pltpu.make_async_copy(src, dst, local_sem.at[index])
        load.start()
        loads.append(load)
    at.meet()
    copies = Copies(send_sem, recv_sem)
    mixer = Mixer(
        at, (conv_w, conv_b, step_b, decay, skip, gain),
        proj, conved, steps, sums, entering, window, gated, squares,
    )
    scatter_refs = (wout, part, from_sib, got, stats, scale)

    gather = Gather(at, copies, inflow, act, weight, acc, proj)
    gather.own(0)
    gather.own(1)
    for load in loads:
        load.wait()

    @pl.when(at.sec == 0)
    def _():
        load = pltpu.make_async_copy(fresh, received, local_sem.at[0])
        load.start()
        load.wait()

    gather.near(0)
    gather.rest()
    mixer.states()
    copies.finish()

    scatter = Scatter(at, copies, mixer, *scatter_refs)
    hops = [copies.make(staged.at[:, columns(p)], received.at[:, columns(p)], at.after) for p in (0, 1)]

    def relay(p):
        scatter.total(p, out.at[0], staged)
        pl.when(at.sec < LAST)(hops[p].start)

    def relayed(p):
        pl.when(at.sec > 0)(hops[p].wait_recv)
        keep = pltpu.make_async_copy(
            received.at[:, columns(p)], act.at[here, columns(p)], local_sem.at[p]
        )
        keep.start()
        gather.own(p)
        return keep

    scatter.first()
    scatter.second()
    relay(0)
    scatter.cross(1)
    scatter.side(1)
    gather = Gather(at, copies, received, act, weight, acc, proj)
    keeps = [relayed(0)]
    scatter.join(1)
    relay(1)
    gather.near(0)
    keeps.append(relayed(1))
    for keep in keeps:
        keep.wait()
    gather.rest()
    mixer.states()
    for p in (0, 1):
        pl.when(at.sec < LAST)(hops[p].wait_send)
    copies.finish()

    scatter = Scatter(at, copies, mixer, *scatter_refs)
    scatter.first()
    scatter.second()
    scatter.total(0, out.at[1], None)
    scatter.cross(1)
    scatter.side(1)
    scatter.join(1)
    scatter.total(1, out.at[1], None)
    copies.finish()


def on_device(
    inflow,
    fresh,
    proj_weight,
    xz_weight,
    conv_weight,
    conv_bias,
    step_bias,
    decay_log,
    skip_weight,
    norm_gain,
    out_weight,
):
    anywhere = pl.BlockSpec(memory_space=pl.ANY)
    vmem = pl.BlockSpec(memory_space=pltpu.VMEM)
    out = pl.pallas_call(
        kernel,
        out_shape=jax.ShapeDtypeStruct((2, ROWS, WIDTH), F32),
        in_specs=[anywhere] * 4 + [vmem] * 7,
        out_specs=vmem,
        scratch_shapes=[
            pltpu.VMEM((TOKENS, WIDTH), BF16),
            pltpu.VMEM((WIDTH, COLS), BF16),
            pltpu.VMEM((TOKENS, COLS), F32),
            pltpu.VMEM((TOKENS, COLS), BF16),
            pltpu.VMEM((TOKENS, 512), BF16),
            pltpu.VMEM((TOKENS, CHAN), F32),
            pltpu.VMEM((TOKENS, CHAN), F32),
            pltpu.VMEM((TOKENS, CHAN), BF16),
            pltpu.VMEM((BLOCK + 8, 512), F32),
            pltpu.VMEM((TOKENS, CHAN), BF16),
            pltpu.VMEM((8, TOKENS), F32),
            pltpu.VMEM((TOKENS, WIDTH), BF16),
            pltpu.VMEM((TOKENS // 2, WIDTH), BF16),
            pltpu.VMEM((2, LAST, ROWS, HALF), BF16),
            pltpu.VMEM((3, 8, TOKENS), F32),
            pltpu.VMEM((TOKENS, 128), F32),
            pltpu.VMEM((ROWS, WIDTH), BF16),
            pltpu.VMEM((ROWS, WIDTH), BF16),
            pltpu.SemaphoreType.DMA((COPIES,)),
            pltpu.SemaphoreType.DMA((COPIES,)),
            pltpu.SemaphoreType.DMA((5,)),
        ],
        compiler_params=pltpu.CompilerParams(
            collective_id=0, has_side_effects=True, vmem_limit_bytes=60 * MIB
        ),
        name="relay_window",
    )(
        inflow[0], fresh[0], xz_weight[0].reshape(WIDTH, 2 * CHAN), proj_weight[0], out_weight[0],
        conv_weight[0], conv_bias, step_bias, decay_log, skip_weight, norm_gain,
    )
    return out[None]


def solution(mesh):
    placed = (
        P("section", "seq", None),
        P(None, "seq", None),
        P("section", None, None),
        P("section", None, None, "seq"),
        P("section", None, None),
        P("section", None),
        P("section", None),
        P("section", None),
        P("section", None),
        P("section", None),
        P("section", "seq", None),
    )
    return jax.shard_map(
        on_device,
        mesh=mesh,
        in_specs=placed,
        out_specs=P("section", None, "seq", None),
        check_vma=False,
    )
```

time: 825 us -> 209 us (0.25)
  waiting for transfers between devices: 433 us -> 0 us
  Pallas kernels: 0 us -> 201 us
  blocking collectives: 133 us -> 0 us
  matrix products: 107 us -> 0 us
  local copies, waits for them, and re-layouts: 109 us -> 7.96 us
  other arithmetic: 21.6 us -> 0 us
  between operations: 13.6 us -> 0.01 us
    reduce_scatter x2 -> x0, waiting for transfers between devices: 286 us -> none  [layer(): lax.psum_scatter(jnp.dot(normed, out_local, preferred_element_type=jnp.fl...]
    pallas_call x0 -> x1, Pallas kernels: none -> 201 us  [on_device(): pl.pallas_call(kernel, out_shape=jax.ShapeDtypeStruct((2, ROWS, WIDTH), F...]
    psum x2 -> x0, blocking collectives: 133 us -> none  [layer(): summed_squares = lax.psum(group_mask * own_squares[None, :], 'seq')]
    all_gather x2 -> x0, waiting for transfers between devices: 132 us -> none  [layer(): lax.all_gather(shard, 'seq', axis=0, tiled=True)]
    dot_general x68 -> x0, matrix products: 107 us -> none  [the longest x2 23.6 us: layer(): jnp.dot(lax.all_gather(shard, 'seq', axis=0, tiled=True), own_weight, pre...]
    dynamic_update_slice x16 -> x0, local copies, waits for them, and re-layouts: 71.3 us -> none  [layer(): lax.scan(run_block, start_state, (x_blocks, b_blocks, c_blocks, step_bloc...]
    dynamic_slice x55 -> x0, local copies, waits for them, and re-layouts: 23.7 us -> none  [the longest x48 14.3 us: layer(): lax.scan(run_block, start_state, (x_blocks, b_blocks, c_blocks, step_bloc...]
    ppermute x1 -> x0, waiting for transfers between devices: 14 us -> none  [shifted(): lax.ppermute(value, axis, [(source, source + steps) for source in range(l...]
  transfers between devices with their start and end apart: 5 -> 0, of which waited for: 5 -> 0; matrix products, arithmetic and copies ran while one was open for 2% -> 0% of each run, Pallas kernels for 0% -> 0%
where the time goes in v2:
time: 209 us
  Pallas kernels  201 us (96%)
  local copies, waits for them, and re-layouts  7.96 us (4%)
    pallas_call x1, Pallas kernels, on_device(): pl.pallas_call(kernel, out_shape=jax.ShapeDtypeStruct((2, ROWS, WIDTH), F...  201 us
    unnamed x2, local copies, waits for them, and re-layouts  7.96 us

profile of v2, /device:TPU:14, one launch (start us, length us, event | category | flops | bytes accessed | tf_op | source)
XLA Modules:
  0.0 208.7 jit_solution(11678172544366407913)
XLA Ops:
  0.0 4.8 %copy.12 = bf16[512,8,2,256]{3,1,2,0:T(8,128)(2,1)} copy(bf16[512,8,2,256]{3,2,1,0:T(2,128)(2,1)} %bitcast.12) | data formatting | bytes 8388608
  4.8 200.7 %relay_window.1 = f32[2,64,4096]{2,1,0:T(8,128)} custom-call(bf16[64,4096]{1,0:T(8,128)(2,1)} %bitcast.14, bf16[64,4096]{1,0:T(8,128)(2,1)} %bitcast.15, bf16[4096,512]{1,0:T(8,128)(2,1)} %bitcast.9, bf16[4096,640]{1,0:T(8,128)(2,1)} %bitcast.11, bf16[256,4096]{1,0:T(8,128)(2,1)} %bitcast.13, f32[4,4608]{1,0:T(4,128)} %bitcast.16, f32[1,4608]{1,0:T(1,128)} %conv_b.1, ...), custom_call_target="tpu_custom_call" | custom-call | tf_op jit(solution)/shard_map/relay_window/pallas_call | solution.py:613
  205.6 3.1 %copy.14 = f32[1,2,64,4096]{3,2,1,0:T(8,128)} copy(f32[1,2,64,4096]{3,2,1,0:T(8,128)} %bitcast.10) | data formatting | bytes 4194304
